TPU v7x, 256 devices: a whole 4x4x8 slice. The times are simulated.
256 devices in a mesh: chan: 8 (over x, z_hi), seq: 32 (over z_lo, y, core).
Axes of the slice: x: 4, y: 4, z: 8 (z_hi: 2, z_lo: 4; z = z_hi * 4 + z_lo), core: 2. Of those that a mesh axis runs over, the one named last changes fastest.
Arguments:
- stream: bfloat16 [512, 1024, 512], P('seq', 'chan'), may hold values from -6 to 6
- weight_value: bfloat16 [512, 512], replicated, may hold values from -0.25 to 0.25
- weight_gate: bfloat16 [512, 512], replicated, may hold values from -0.25 to 0.25
- weight_out: bfloat16 [512, 512], replicated, may hold values from -0.25 to 0.25
- within_factor: bfloat16 [1024, 1024], replicated, may hold values from -0.1875 to 0.1875
- across_factor: bfloat16 [512, 512], replicated, may hold values from -0.25 to 0.25
- within_scale: bfloat16 [1024, 512], P(None, 'chan'), may hold values from -4 to 4
- across_scale: bfloat16 [512, 512], P(None, 'chan'), may hold values from -4 to 4
- mix_gain: bfloat16 [512], replicated, may hold values from 0.099609375 to 1.8984375
- final_gain: bfloat16 [512], replicated, may hold values from 0.099609375 to 1.8984375
- block_up: bfloat16 [4, 128, 512], replicated, may hold values from -0.5 to 0.5
- block_down: bfloat16 [4, 512, 128], replicated, may hold values from -0.25 to 0.25
Outputs:
- result: bfloat16 [512, 1024, 512], P('seq', 'chan')
All inputs are finite; a program needn't handle non-finite values.
Results may differ from a plain program's by a relative error of at most 0.015.
Values may be sent and summed in bfloat16 or wider, within the bound.
A program may use at most 128 MiB of HBM per device.

v0:
```python
import jax
import jax.numpy as jnp
from jax import lax
from jax.sharding import PartitionSpec as P

eps = 1e-05


def rms_scale(flat, gain):
    power = jnp.mean(flat * flat, axis=-1, keepdims=True)
    return flat * lax.rsqrt(power + eps) * gain.astype(jnp.float32)


def body(
    stream,
    weight_value,
    weight_gate,
    weight_out,
    within_factor,
    across_factor,
    within_scale,
    across_scale,
    mix_gain,
    final_gain,
    block_up,
    block_down,
):
    rows_a, rows_b, width = stream.shape
    flat = stream.reshape(rows_a * rows_b, width)
    normed = rms_scale(flat.astype(jnp.float32), mix_gain).astype(jnp.bfloat16)
    values = (
        jnp.dot(normed, weight_value, preferred_element_type=jnp.float32)
        .astype(jnp.bfloat16)
        .reshape(rows_a, rows_b, width)
    )
    gates = (
        jnp.dot(normed, weight_gate, preferred_element_type=jnp.float32)
        .astype(jnp.bfloat16)
        .reshape(rows_a, rows_b, width)
    )
    lower_within = jnp.tril(within_factor)
    lower_across = jnp.tril(across_factor)
    scale_rows = across_scale.astype(jnp.float32)[:, None, :]
    first = jnp.einsum(
        "pb,abc->apc",
        lower_within,
        lax.all_to_all(values, "chan", split_axis=2, concat_axis=1, tiled=True),
        preferred_element_type=jnp.float32,
    )
    spread = (first * within_scale.astype(jnp.float32)[None]).astype(jnp.bfloat16)
    summed = jnp.einsum(
        "qa,abc->qbc",
        lower_across,
        lax.all_to_all(spread, "seq", split_axis=1, concat_axis=0, tiled=True),
        preferred_element_type=jnp.float32,
    )
    carried = (summed * scale_rows).astype(jnp.bfloat16)
    landed = lax.all_to_all(
        lax.all_to_all(carried, "seq", split_axis=0, concat_axis=1, tiled=True),
        "chan",
        split_axis=1,
        concat_axis=2,
        tiled=True,
    )
    gated = (gates.astype(jnp.float32) * landed.astype(jnp.float32)).astype(jnp.bfloat16)
    gated_flat = gated.reshape(rows_a * rows_b, width)
    middle = (
        flat.astype(jnp.float32)
        + jnp.dot(gated_flat, weight_out, preferred_element_type=jnp.float32)
    ).astype(jnp.bfloat16)
    renormed = rms_scale(middle.astype(jnp.float32), final_gain).astype(jnp.bfloat16)
    blocks = block_up.shape[0]
    split = renormed.reshape(rows_a * rows_b, blocks, width // blocks)
    inner = jax.nn.gelu(
        jnp.einsum("tkd,kdh->tkh", split, block_up, preferred_element_type=jnp.float32),
        approximate=True,
    ).astype(jnp.bfloat16)
    outer = jnp.einsum(
        "tkh,khd->tkd", inner, block_down, preferred_element_type=jnp.float32
    ).reshape(rows_a * rows_b, width)
    result = (middle.astype(jnp.float32) + outer).astype(jnp.bfloat16)
    return result.reshape(rows_a, rows_b, width)


def solution(mesh):
    placed = (
        P("seq", "chan", None),
        P(),
        P(),
        P(),
        P(),
        P(),
        P(None, "chan"),
        P(None, "chan"),
        P(),
        P(),
        P(),
        P(),
    )
    return jax.shard_map(
        body, mesh=mesh, in_specs=placed, out_specs=P("seq", "chan", None), check_vma=False
    )
```

profile of v0, /device:TPU:33, one launch (start us, length us, event | category | flops | bytes accessed | tf_op | source)
XLA Modules:
  0.0 372.9 jit_solution(14415880274985513532)
XLA Ops:
  2.2 4.2 %copy.68 = f32[2048,512]{0,1:T(8,128)} copy(bf16[2048,512]{1,0:T(8,128)(2,1)} %bitcast.72) | data formatting | bytes 6291456 | tf_op jit(solution)/shard_map/convert_element_type | solution.py:68
  6.4 3.6 convolution_convert_fusion
  10.0 3.1 copy.50
  13.0 9.7 %all-to-all-start = ((bf16[16,128,512]{1,0,2:T(8,128)(2,1)}), bf16[16,128,512]{1,0,2:T(8,128)(2,1)S(1)}, u32[]{:S(2)}, u32[]{:S(2)}) async-start(bf16[16,128,512]{1,0,2:T(8,128)(2,1)} %copy.50), calls=%async_computation | async-start | bytes 4194304 | tf_op jit(solution)/shard_map/all_to_all | solution.py:47
  22.8 52.8 %all-to-all-done = bf16[16,128,512]{1,0,2:T(8,128)(2,1)S(1)} async-done(((bf16[16,128,512]{1,0,2:T(8,128)(2,1)}), bf16[16,128,512]{1,0,2:T(8,128)(2,1)S(1)}, u32[]{:S(2)}, u32[]{:S(2)}) %all-to-all-start) | async-done | bytes 2097184 | tf_op jit(solution)/shard_map/all_to_all | solution.py:47
  75.6 2.7 copy.52
  78.3 4.1 %all_to_all.49 = bf16[16,1024,64]{1,2,0:T(8,128)(2,1)} reshape(bf16[16,8,128,64]{2,1,3,0:T(8,128)(2,1)} %copy.52) | data formatting | bytes 4194304 | tf_op jit(solution)/shard_map/all_to_all | solution.py:47
  82.4 4.6 %fusion.16 = bf16[16,1024,64]{1,2,0:T(8,128)(2,1)S(1)} fusion(bf16[16,1024,64]{1,2,0:T(8,128)(2,1)} %all_to_all.49, bf16[1024,1024]{1,0:T(8,128)(2,1)} %param.16, f32[1024,64]{0,1:T(8,128)S(1)} %convert_element_type.82), kind=kOutput, calls=%fused_computation.19 | convolution fusion | flops 2151677952 | bytes 6553600 | tf_op jit(solution)/shard_map/pb,abc->apc/dot_general | solution.py:44
  87.0 4.9 %copy.53 = bf16[16,1024,64]{2,0,1:T(8,128)(2,1)} copy(bf16[16,1024,64]{1,2,0:T(8,128)(2,1)S(1)} %fusion.16) | data formatting | bytes 4194304 | tf_op jit(solution)/shard_map/convert_element_type | solution.py:50
  91.9 7.9 %reshape.62 = bf16[32,2,16384]{2,1,0:T(2,128)(2,1)} reshape(bf16[1024,16,64]{2,1,0:T(8,128)(2,1)} %bitcast.63) | data formatting | bytes 4194304
  99.8 7.6 %all-to-all-start.1 = ((bf16[32,2,16384]{2,1,0:T(2,128)(2,1)}), bf16[32,2,16384]{2,1,0:T(2,128)(2,1)S(1)}, u32[]{:S(2)}, u32[]{:S(2)}) async-start(bf16[32,2,16384]{2,1,0:T(2,128)(2,1)} %reshape.62), calls=%async_computation.1 | async-start | bytes 4194304 | tf_op jit(solution)/shard_map/all_to_all | solution.py:54
  107.5 48.6 %all-to-all-done.1 = bf16[32,2,16384]{2,1,0:T(2,128)(2,1)S(1)} async-done(((bf16[32,2,16384]{2,1,0:T(2,128)(2,1)}), bf16[32,2,16384]{2,1,0:T(2,128)(2,1)S(1)}, u32[]{:S(2)}, u32[]{:S(2)}) %all-to-all-start.1) | async-done | bytes 2097184 | tf_op jit(solution)/shard_map/all_to_all | solution.py:54
  156.1 4.0 %reshape.63 = bf16[1024,16,64]{2,1,0:T(8,128)(2,1)} reshape(bf16[32,2,16384]{2,1,0:T(2,128)(2,1)S(1)} %all-to-all-done.1) | data formatting | bytes 4194304
  160.1 5.2 %copy.55 = bf16[32,16,32,64]{3,2,1,0:T(8,128)(2,1)} copy(bf16[32,16,32,64]{3,1,2,0:T(8,128)(2,1)} %bitcast.65) | data formatting | bytes 4194304 | tf_op jit(solution)/shard_map/all_to_all | solution.py:54
  165.3 4.5 %copy.56 = bf16[512,32,64]{0,2,1:T(8,128)(2,1)S(1)} copy(bf16[512,32,64]{2,1,0:T(8,128)(2,1)} %bitcast.66) | data formatting | bytes 4194304 | tf_op jit(solution)/shard_map/all_to_all | solution.py:54
  171.8 6.7 %copy.57 = bf16[512,32,64]{2,1,0:T(8,128)(2,1)} copy(bf16[512,32,64]{0,2,1:T(8,128)(2,1)S(1)} %multiply_convert_fusion.1) | data formatting | bytes 4194304 | tf_op jit(solution)/shard_map/convert_element_type | solution.py:57
  178.4 6.8 %reshape.64 = bf16[32,2,16384]{2,1,0:T(2,128)(2,1)S(1)} reshape(bf16[512,32,64]{2,1,0:T(8,128)(2,1)} %copy.57) | data formatting | bytes 4194304
  185.3 55.0 %all_to_all.63 = bf16[32,2,16384]{2,1,0:T(2,128)(2,1)} all-to-all(bf16[32,2,16384]{2,1,0:T(2,128)(2,1)S(1)} %reshape.64), channel_id=1, replica_groups=mesh['chan'=8,'seq'=32] {'seq'}, dimensions={0} | all-to-all | bytes 4194304 | tf_op jit(solution)/shard_map/all_to_all | solution.py:59
  240.3 7.9 %reshape.65 = bf16[512,32,64]{2,1,0:T(8,128)(2,1)} reshape(bf16[32,2,16384]{2,1,0:T(2,128)(2,1)} %all_to_all.63) | data formatting | bytes 4194304
  248.2 3.3 copy.58
  251.5 4.7 %copy.76 = bf16[16,1024,64]{2,0,1:T(8,128)(2,1)} copy(bf16[16,1024,64]{2,1,0:T(8,128)(2,1)S(1)} %bitcast.68) | data formatting | bytes 4194304 | tf_op jit(solution)/shard_map/all_to_all | solution.py:59
  256.1 7.6 %reshape.66 = bf16[8,2,65536]{2,1,0:T(2,128)(2,1)} reshape(bf16[1024,16,64]{2,1,0:T(8,128)(2,1)} %bitcast.69) | data formatting | bytes 4194304
  263.7 3.8 %all-to-all-start.3 = ((bf16[8,2,65536]{2,1,0:T(2,128)(2,1)}), bf16[8,2,65536]{2,1,0:T(2,128)(2,1)S(1)}, u32[]{:S(2)}, u32[]{:S(2)}) async-start(bf16[8,2,65536]{2,1,0:T(2,128)(2,1)} %reshape.66), calls=%async_computation.3 | async-start | bytes 4194304 | tf_op jit(solution)/shard_map/all_to_all | solution.py:58
  267.6 52.9 %all-to-all-done.3 = bf16[8,2,65536]{2,1,0:T(2,128)(2,1)S(1)} async-done(((bf16[8,2,65536]{2,1,0:T(2,128)(2,1)}), bf16[8,2,65536]{2,1,0:T(2,128)(2,1)S(1)}, u32[]{:S(2)}, u32[]{:S(2)}) %all-to-all-start.3) | async-done | bytes 2097184 | tf_op jit(solution)/shard_map/all_to_all | solution.py:58
  320.5 5.0 %reshape.67 = bf16[1024,16,64]{2,1,0:T(8,128)(2,1)} reshape(bf16[8,2,65536]{2,1,0:T(2,128)(2,1)S(1)} %all-to-all-done.3) | data formatting | bytes 4194304
  325.4 4.5 %copy.60 = bf16[16,1024,64]{1,2,0:T(8,128)(2,1)S(1)} copy(bf16[16,1024,64]{2,0,1:T(8,128)(2,1)} %bitcast.64) | data formatting | bytes 4194304 | tf_op jit(solution)/shard_map/all_to_all | solution.py:58
  330.4 2.9 copy.74
  333.3 6.9 %copy.71 = f32[16,128,8,64]{3,2,1,0:T(8,128)} copy(f32[16,128,8,64]{1,2,3,0:T(8,128)} %bitcast.62) | data formatting | bytes 8388608 | tf_op jit(solution)/shard_map/convert_element_type | solution.py:65
  340.2 7.5 %reshape.61 = f32[2048,512]{1,0:T(8,128)} reshape(f32[16,128,8,64]{3,2,1,0:T(8,128)} %copy.71) | data formatting | bytes 8388608 | tf_op jit(solution)/shard_map/convert_element_type | solution.py:65
  347.8 7.3 %fusion.12 = (f32[2048]{0:T(1024)S(1)}, bf16[2048,512]{0,1:T(8,128)(2,1)S(1)}) fusion(f32[2048,512]{0,1:T(8,128)} %copy.68, bf16[512,512]{1,0:T(8,128)(2,1)S(1)} %copy-done, f32[2048,512]{1,0:T(8,128)} %reshape.61, bf16[512,512]{1,0:T(8,128)(2,1)S(1)} %copy-done.8, f32[512]{0:T(512)S(1)} %convert_element_type.77, f32[2048]{0:T(1024)S(1)} %rsqrt_bitcast_fusion), kind=kOutput, calls=%fused_computation.14 | convolution fusion | flops 2160064512 | bytes 11552768 | tf_op jit(solution)/shard_map/dot_general | solution.py:69
  357.1 9.8 %fusion.8 = f32[4,2048,128]{1,2,0:T(8,128)} fusion(bf16[4,512,128]{2,1,0:T(8,128)(2,1)S(1)} %copy-done.9, bf16[2048,4,128]{0,2,1:T(8,128)(2,1)} %bitcast.76, bf16[4,128,512]{2,1,0:T(8,128)(2,1)} %param.22), kind=kOutput, calls=%fused_computation.9 | convolution fusion | flops 2185232384 | bytes 7340032 | tf_op jit(solution)/shard_map/tkh,khd->tkd/dot_general | solution.py:78
  366.9 3.5 fusion.15
  (32 shorter events, 9.1 us)
Async XLA Ops:
  0.0 347.8 %copy-start = (bf16[512,512]{1,0:T(8,128)(2,1)S(1)}, bf16[512,512]{1,0:T(8,128)(2,1)}, u32[]{:S(2)}) copy-start(bf16[512,512]{1,0:T(8,128)(2,1)} %param.15) | copy-start | bytes 1572868
  0.0 6.3 %copy-start.5 = (bf16[512]{0:T(512)(128)(2,1)S(1)}, bf16[512]{0:T(512)(128)(2,1)}, u32[]{:S(2)}) copy-start(bf16[512]{0:T(512)(128)(2,1)} %param.20) | copy-start | bytes 3076
  0.0 6.4 %copy-start.7 = (bf16[512,512]{1,0:T(8,128)(2,1)S(1)}, bf16[512,512]{1,0:T(8,128)(2,1)}, u32[]{:S(2)}) copy-start(bf16[512,512]{1,0:T(8,128)(2,1)} %param.13) | copy-start | bytes 1572868
  10.0 12.8 %copy-start.3 = (bf16[1024,64]{0,1:T(8,128)(2,1)S(1)}, bf16[1024,64]{0,1:T(8,128)(2,1)}, u32[]{:S(2)}) copy-start(bf16[1024,64]{0,1:T(8,128)(2,1)} %param.18) | copy-start | bytes 393220
  13.0 62.5 %all-to-all-start = ((bf16[16,128,512]{1,0,2:T(8,128)(2,1)}), bf16[16,128,512]{1,0,2:T(8,128)(2,1)S(1)}, u32[]{:S(2)}, u32[]{:S(2)}) async-start(bf16[16,128,512]{1,0,2:T(8,128)(2,1)} %copy.50), calls=%async_computation | async-start | bytes 4194304 | tf_op jit(solution)/shard_map/all_to_all | solution.py:47
  91.9 15.6 %copy-start.4 = (bf16[512,64]{0,1:T(8,128)(2,1)S(1)}, bf16[512,64]{0,1:T(8,128)(2,1)}, u32[]{:S(2)}) copy-start(bf16[512,64]{0,1:T(8,128)(2,1)} %param.19) | copy-start | bytes 196612
  99.8 56.3 %all-to-all-start.1 = ((bf16[32,2,16384]{2,1,0:T(2,128)(2,1)}), bf16[32,2,16384]{2,1,0:T(2,128)(2,1)S(1)}, u32[]{:S(2)}, u32[]{:S(2)}) async-start(bf16[32,2,16384]{2,1,0:T(2,128)(2,1)} %reshape.62), calls=%async_computation.1 | async-start | bytes 4194304 | tf_op jit(solution)/shard_map/all_to_all | solution.py:54
  165.3 4.5 %copy-start.2 = (bf16[512,512]{1,0:T(8,128)(2,1)S(1)}, bf16[512,512]{1,0:T(8,128)(2,1)}, u32[]{:S(2)}) copy-start(bf16[512,512]{1,0:T(8,128)(2,1)} %param.17) | copy-start | bytes 1572868
  256.1 11.4 %copy-start.6 = (bf16[512]{0:T(512)(128)(2,1)S(1)}, bf16[512]{0:T(512)(128)(2,1)}, u32[]{:S(2)}) copy-start(bf16[512]{0:T(512)(128)(2,1)} %param.21) | copy-start | bytes 3076
  263.7 56.8 %all-to-all-start.3 = ((bf16[8,2,65536]{2,1,0:T(2,128)(2,1)}), bf16[8,2,65536]{2,1,0:T(2,128)(2,1)S(1)}, u32[]{:S(2)}, u32[]{:S(2)}) async-start(bf16[8,2,65536]{2,1,0:T(2,128)(2,1)} %reshape.66), calls=%async_computation.3 | async-start | bytes 4194304 | tf_op jit(solution)/shard_map/all_to_all | solution.py:58
  340.2 7.5 %copy-start.8 = (bf16[512,512]{1,0:T(8,128)(2,1)S(1)}, bf16[512,512]{1,0:T(8,128)(2,1)}, u32[]{:S(2)}) copy-start(bf16[512,512]{1,0:T(8,128)(2,1)} %param.14) | copy-start | bytes 1572868
  355.1 2.0 copy-start.1
  355.1 2.0 copy-start.9
where the time goes:
time: 374 us; the launch traced here: 373 us
  waiting for transfers between devices  154 us (41%)
  local copies, waits for them, and re-layouts  107 us (29%)
  blocking collectives  55 us (15%)
  matrix products  26.6 us (7%)
  starting transfers between devices  21.2 us (6%)
  other arithmetic  8.63 us (2%)
    all_to_all x1, blocking collectives, body(): lax.all_to_all(carried, 'seq', split_axis=0, concat_axis=1, tiled=True)  55 us
    all_to_all x1, waiting for transfers between devices, body(): lax.all_to_all(lax.all_to_all(carried, 'seq', split_axis=0, concat_axis=1...  52.9 us
    all_to_all x1, waiting for transfers between devices, body(): lax.all_to_all(values, 'chan', split_axis=2, concat_axis=1, tiled=True)  52.8 us
    all_to_all x1, waiting for transfers between devices, body(): lax.all_to_all(spread, 'seq', split_axis=1, concat_axis=0, tiled=True)  48.6 us
    unnamed x27, local copies, waits for them, and re-layouts  42.3 us
    convert_element_type x2, local copies, waits for them, and re-layouts, body(): landed.astype(jnp.float32)  14.4 us
    dot_general x1, matrix products, body(): jnp.einsum('tkh,khd->tkd', inner, block_down, preferred_element_type=jnp....  9.78 us
    all_to_all x2, local copies, waits for them, and re-layouts, body(): lax.all_to_all(spread, 'seq', split_axis=1, concat_axis=0, tiled=True)  9.75 us
  transfers between devices with their start and end apart: 3, of which 3 were waited for; matrix products, arithmetic and copies ran while one was open for 0% of the time, Pallas kernels for 0%

commit v1 on v0

v1 whole, which is shorter than its diff:
```python
import jax
import jax.numpy as jnp
from jax import lax
from jax.experimental import pallas as pl
from jax.experimental.pallas import tpu as pltpu
from jax.sharding import PartitionSpec as P

eps = 1e-05
MESH = pl.DeviceIdType.MESH
F32 = jnp.float32
BF16 = jnp.bfloat16
NX, NZ, NY, NC = 4, 8, 4, 2
LAST = (((1,), (1,)), ((), ()))
FIRST = (((0,), (0,)), ((), ()))


def dot(left, right, dims=None):
    if dims is None:
        return jnp.dot(left, right, preferred_element_type=F32)
    return lax.dot_general(left, right, dims, preferred_element_type=F32)


def rms(flat, gain):
    power = jnp.mean(flat * flat, axis=-1, keepdims=True)
    return flat * lax.rsqrt(power + eps) * gain


def gelu(h):
    cdf = 0.5 * (1.0 + jnp.tanh(0.7978845608028654 * (h + 0.044715 * (h * h * h))))
    return h * cdf


def place(x, z, y, core):
    return x * 2 + z // 4, (z % 4) * 8 + y * 2 + core


def kernel(
    stream_hbm, wv_hbm, wg_hbm, wo_hbm, within_hbm, across_hbm, ws_hbm, as_hbm,
    mix_hbm, final_hbm, up_hbm, down_hbm,
    out_hbm,
    stream, wv, wg, wo, within, across, ws, ascale, mix_gain, final_gain, up, down,
    wvt, wgt, wst, normed, gates,
    send1, recv1, send2, recv2, send3, recv3, flip1, flip2, result,
    in_sem, out_sem, s1, r1, s2, r2, s3, r3,
):
    chan = lax.axis_index("chan")
    seq = lax.axis_index("seq")
    x, z = chan // 2, (chan % 2) * 4 + seq // 8
    y, core = (seq // 2) % 4, seq % 2
    zl, yc = seq // 8, seq % 8
    own = x * 8 + z

    def p_block(half, y_of, core_of):
        return 2 * ((x + y_of + 2 * core_of + half) % NX) + core_of

    def load(number, source, target):
        return pltpu.make_async_copy(source, target, in_sem.at[number])

    loads = [
        load(0, stream_hbm, stream), load(1, wv_hbm, wv), load(2, mix_hbm, mix_gain),
        load(3, wg_hbm, wg), load(4, within_hbm, within), load(5, ws_hbm, ws),
        load(6, across_hbm, across), load(7, as_hbm, ascale), load(8, wo_hbm, wo),
        load(9, final_hbm, final_gain), load(10, up_hbm, up), load(11, down_hbm, down),
    ]
    for one in loads:
        one.start()

    barrier = pltpu.get_barrier_semaphore()

    def greet(x_of, z_of, y_of, core_of):
        pl.semaphore_signal(
            barrier, inc=1, device_id=place(x_of, z_of, y_of, core_of), device_id_type=MESH
        )

    @pl.loop(1, NX * NZ)
    def _(i):
        greet((x + i // NZ) % NX, (z + i % NZ) % NZ, y, core)

    @pl.loop(1, NY * NC)
    def _(i):
        greet(x, z, (y + i // NC) % NY, (core + i % NC) % NC)

    for half in range(2):
        @pl.loop(0, NX * NZ)
        def _(i):
            x_of = i // NZ
            core_of = chan % 2
            greet(x_of, i % NZ, (x - x_of - 2 * core_of - half + 2 * NX) % NY, core_of)

    for number in (1, 2):
        loads[number].wait()
    wvt[...] = wv[...].astype(F32).T.reshape(32, 2, 8, 512).swapaxes(0, 1).reshape(2, 256, 512).astype(BF16)
    loads[0].wait()
    gain = mix_gain[...].astype(F32)

    def values(half, pair, tokens):
        found = dot(wvt[half], tokens, LAST)
        split = [found[:, :128].reshape(32, 8, 128), found[:, 128:].reshape(32, 8, 128)]
        send1[half, :, pair] = jnp.concatenate(split, axis=1).astype(BF16)

    @pl.loop(0, 8)
    def _(pair):
        flat = stream[pl.ds(2 * pair, 2)].reshape(256, 512).astype(F32)
        tokens = rms(flat, gain).astype(BF16)
        normed[pair] = tokens
        values(0, pair, tokens)

    def send_values(half):
        pltpu.make_async_copy(send1.at[half, own], recv1.at[half, chan, zl], r1.at[half]).start()

        @pl.loop(1, NX * NZ)
        def _(i):
            x_of, z_of = (x + i // NZ) % NX, (z + i % NZ) % NZ
            pltpu.make_async_remote_copy(
                send1.at[half, x_of * 8 + z_of], recv1.at[half, chan, zl],
                s1.at[half], r1.at[half],
                device_id=place(x_of, z_of, y, core), device_id_type=MESH,
            ).start()

    pl.semaphore_wait(barrier, NX * NZ - 1 + NY * NC - 1 + 2 * NX * NZ)
    send_values(0)

    @pl.loop(0, 8)
    def _(pair):
        values(1, pair, normed[pair])

    send_values(1)

    loads[3].wait()
    wgt[...] = wg[...].astype(F32).T.astype(BF16)

    @pl.loop(0, 8)
    def _(pair):
        found = dot(wgt[...], normed[pair], LAST).astype(BF16)
        gates[2 * pair] = found[:, :128]
        gates[2 * pair + 1] = found[:, 128:]

    for number in range(4, 12):
        loads[number].wait()
    lower = lax.broadcasted_iota(jnp.int32, (256, 256), 0) >= lax.broadcasted_iota(jnp.int32, (256, 256), 1)
    for n in range(4):
        edge = pl.ds(256 * n, 256)
        within[edge, edge] = jnp.where(lower, within[edge, edge].astype(F32), 0.0).astype(BF16)
    for n in range(2):
        edge = pl.ds(256 * n, 256)
        across[edge, edge] = jnp.where(lower, across[edge, edge].astype(F32), 0.0).astype(BF16)
    picked = lax.broadcasted_iota(jnp.int32, (16, 64), 1) == 16 * zl + lax.broadcasted_iota(jnp.int32, (16, 64), 0)
    wst[...] = dot(picked.astype(F32).astype(BF16), ws[...], LAST)

    def middle_of(half):
        pltpu.make_async_copy(recv1.at[half], recv1.at[half], r1.at[half]).wait()
        for n in range(4):
            blocks = [recv1[half, k].reshape(512, 128) for k in range(2 * n + 2)]
            found = dot(
                jnp.concatenate(blocks, axis=1), within[pl.ds(256 * n, 256), pl.ds(0, 256 * (n + 1))], LAST
            )
            scale = wst[pl.ds(8 * half, 8), pl.ds(256 * n, 256)]
            scaled = (found.reshape(64, 8, 256) * scale[None]).reshape(512, 256)
            for side in range(2):
                flip1[side] = scaled[:, 128 * side : 128 * side + 128]
            for side in range(2):
                for c in range(8):
                    column = flip1[side, pl.ds(c, 64, stride=8), :]
                    send2[half, 2 * n + side, c] = column.astype(BF16).reshape(4, 16, 128)
        pltpu.make_async_copy(
            send2.at[half, p_block(half, y, core)], recv2.at[half, :, :, yc], r2.at[half]
        ).start()

        @pl.loop(1, NY * NC)
        def _(i):
            y_of, core_of = (y + i // NC) % NY, (core + i % NC) % NC
            pltpu.make_async_remote_copy(
                send2.at[half, p_block(half, y_of, core_of)], recv2.at[half, :, :, yc],
                s2.at[half], r2.at[half],
                device_id=place(x, z, y_of, core_of), device_id_type=MESH,
            ).start()

    def across_of(half):
        pltpu.make_async_copy(recv2.at[half], recv2.at[half], r2.at[half]).wait()
        for c in range(0, 8, 2):
            both = jnp.concatenate(
                [recv2[half, c].reshape(512, 128), recv2[half, c + 1].reshape(512, 128)], axis=1
            )
            row = lax.broadcasted_iota(jnp.int32, (64, 256), 0)
            wanted = 16 * zl + 8 * half + c + lax.broadcasted_iota(jnp.int32, (64, 256), 1) // 128
            spread = (row == wanted).astype(F32).astype(BF16)
            for n in range(2):
                rows = pl.ds(256 * n, 256)
                found = dot(across[rows, pl.ds(0, 256 * (n + 1))], both[: 256 * (n + 1)])
                found = found * dot(ascale[rows, :], spread)
                for side in range(2):
                    flip2[pl.ds(2048 * n + c + side, 256, stride=8), :] = found[:, 128 * side : 128 * side + 128]

        @pl.loop(0, 32)
        def _(block):
            start = pl.multiple_of(block * 128, 128)
            send3[half, block] = flip2[pl.ds(start, 128), :].reshape(8, 16, 128).astype(BF16)

    def send_mixed(half, first, count, sem):
        block = p_block(half, y, core)
        rows = pl.ds(first, count)

        def remote(i):
            zl_of, yc_of = (zl + i % 4) % 4, (yc + i // 4) % 8
            seq_of = zl_of * 8 + yc_of
            pltpu.make_async_remote_copy(
                send3.at[half, seq_of, rows], recv3.at[half, rows, own],
                s3.at[sem], r3.at[sem], device_id=(block, seq_of), device_id_type=MESH,
            ).start()

        @pl.when(block == chan)
        def _():
            pltpu.make_async_copy(
                send3.at[half, seq, rows], recv3.at[half, rows, own], r3.at[sem]
            ).start()

        @pl.when(block != chan)
        def _():
            remote(0)

        @pl.loop(1, 32)
        def _(i):
            remote(i)

    middle_of(0)
    across_of(0)
    send_mixed(0, 0, 8, 4)
    middle_of(1)
    across_of(1)
    for part in range(4):
        send_mixed(1, 2 * part, 2, part)

    pltpu.make_async_copy(recv3.at[0], recv3.at[0], r3.at[4]).wait()
    gain2 = final_gain[...].astype(F32)
    for part in range(4):
        arrived = recv3.at[1, pl.ds(2 * part, 2)]
        pltpu.make_async_copy(arrived, arrived, r3.at[part]).wait()

        @pl.loop(2 * part, 2 * part + 2)
        def _(pair):
            halves = [recv3[half, pair].astype(F32) for half in range(2)]
            projected = []
            for one in range(2):
                mixed = jnp.concatenate([h[:, 8 * one : 8 * one + 8] for h in halves], axis=1)
                gated = mixed.reshape(512, 128) * gates[2 * pair + one].astype(F32)
                projected.append(dot(gated.astype(BF16), wo[...], FIRST))
            flat = stream[pl.ds(2 * pair, 2)].reshape(256, 512).astype(F32)
            middle = (flat + jnp.concatenate(projected, axis=0)).astype(BF16).astype(F32)
            renormed = rms(middle, gain2).astype(BF16)
            outer = []
            for k in range(4):
                inner = gelu(dot(renormed[:, 128 * k : 128 * k + 128], up[k])).astype(BF16)
                outer.append(dot(inner, down[k]))
            total = (middle + jnp.concatenate(outer, axis=1)).astype(BF16)
            result[pl.ds(2 * pair, 2)] = total.reshape(2, 128, 512)

        rows = pl.ds(4 * part, 4)
        pltpu.make_async_copy(result.at[rows], out_hbm.at[rows], out_sem.at[part]).start()

    for half in range(2):
        sent = send1.at[half, pl.ds(0, 31)]
        pltpu.make_async_copy(sent, sent, s1.at[half]).wait()
        sent = send2.at[half, pl.ds(0, 7)]
        pltpu.make_async_copy(sent, sent, s2.at[half]).wait()
    for sem in range(5):
        rows = pl.ds(0, 8) if sem == 4 else pl.ds(2 * sem, 2)
        half = 0 if sem == 4 else 1
        rest = send3.at[half, pl.ds(1, 31), rows]
        pltpu.make_async_copy(rest, rest, s3.at[sem]).wait()

        @pl.when(p_block(half, y, core) != chan)
        def _():
            one = send3.at[half, 0, rows]
            pltpu.make_async_copy(one, one, s3.at[sem]).wait()

    for part in range(4):
        rows = pl.ds(4 * part, 4)
        pltpu.make_async_copy(result.at[rows], out_hbm.at[rows], out_sem.at[part]).wait()


def body(
    stream, weight_value, weight_gate, weight_out, within_factor, across_factor,
    within_scale, across_scale, mix_gain, final_gain, block_up, block_down,
):
    args = (
        stream, weight_value, weight_gate, weight_out, within_factor, across_factor,
        within_scale, across_scale, mix_gain.reshape(1, -1), final_gain.reshape(1, -1),
        block_up, block_down,
    )
    anywhere = pl.BlockSpec(memory_space=pl.ANY)
    return pl.pallas_call(
        kernel,
        out_shape=jax.ShapeDtypeStruct(stream.shape, BF16),
        in_specs=[anywhere] * len(args),
        out_specs=anywhere,
        scratch_shapes=[pltpu.VMEM(a.shape, BF16) for a in args] + [
            pltpu.VMEM((2, 256, 512), BF16),
            pltpu.VMEM((512, 512), BF16),
            pltpu.VMEM((16, 1024), F32),
            pltpu.VMEM((8, 256, 512), BF16),
            pltpu.VMEM((16, 512, 128), BF16),
            pltpu.VMEM((2, 32, 8, 16, 128), BF16),
            pltpu.VMEM((2, 8, 4, 8, 16, 128), BF16),
            pltpu.VMEM((2, 8, 8, 4, 16, 128), BF16),
            pltpu.VMEM((2, 8, 4, 8, 16, 128), BF16),
            pltpu.VMEM((2, 32, 8, 16, 128), BF16),
            pltpu.VMEM((2, 8, 32, 16, 128), BF16),
            pltpu.VMEM((2, 512, 128), F32),
            pltpu.VMEM((4096, 128), F32),
            pltpu.VMEM((16, 128, 512), BF16),
            pltpu.SemaphoreType.DMA((12,)),
            pltpu.SemaphoreType.DMA((4,)),
            pltpu.SemaphoreType.DMA((2,)),
            pltpu.SemaphoreType.DMA((2,)),
            pltpu.SemaphoreType.DMA((2,)),
            pltpu.SemaphoreType.DMA((2,)),
            pltpu.SemaphoreType.DMA((5,)),
            pltpu.SemaphoreType.DMA((5,)),
        ],
        compiler_params=pltpu.CompilerParams(
            collective_id=0, has_side_effects=True, vmem_limit_bytes=56 * 2**20
        ),
        cost_estimate=pl.CostEstimate(
            flops=9 * 10**9, bytes_accessed=12 * 2**20, transcendentals=2**22
        ),
        name="mixer",
    )(*args)


def solution(mesh):
    placed = (
        P("seq", "chan", None), P(), P(), P(), P(), P(), P(None, "chan"), P(None, "chan"),
        P(), P(), P(), P(),
    )
    return jax.shard_map(
        body, mesh=mesh, in_specs=placed, out_specs=P("seq", "chan", None), check_vma=False
    )
```

time: 374 us -> 133 us (0.36)
  the two profiles are of different devices: /device:TPU:33 before, /device:TPU:1 now
where the time goes in v1:
time: 133 us
  Pallas kernels  124 us (93%)
  local copies, waits for them, and re-layouts  8.96 us (7%)
    pallas_call x1, Pallas kernels, body(): pl.pallas_call(kernel, out_shape=jax.ShapeDtypeStruct(stream.shape, BF16)...  124 us
    unnamed x3, local copies, waits for them, and re-layouts  6.43 us

profile of v1, /device:TPU:1, one launch (start us, length us, event | category | flops | bytes accessed | tf_op | source)
XLA Modules:
  0.0 133.0 jit_solution(15248725594637502713)
XLA Ops:
  0.0 1.3 reshape.6.mix_hbm
  1.3 1.3 reshape.7.final_hbm
  2.5 1.6 %copy.14.as_hbm = bf16[512,64]{1,0:T(8,128)(2,1)} copy(bf16[512,64]{0,1:T(8,128)(2,1)} %param.19) | data formatting | bytes 131072 | tf_op args[7]
  4.1 1.7 %copy.13.ws_hbm = bf16[1024,64]{1,0:T(8,128)(2,1)} copy(bf16[1024,64]{0,1:T(8,128)(2,1)} %param.18) | data formatting | bytes 262144 | tf_op args[6]
  5.9 124.1 %mixer.1 = bf16[16,128,512]{2,1,0:T(8,128)(2,1)} custom-call(bf16[16,128,512]{2,1,0:T(8,128)(2,1)} %stream_hbm.1, bf16[512,512]{1,0:T(8,128)(2,1)} %wv_hbm.1, bf16[512,512]{1,0:T(8,128)(2,1)} %wg_hbm.1, bf16[512,512]{1,0:T(8,128)(2,1)} %wo_hbm.1, bf16[1024,1024]{1,0:T(8,128)(2,1)} %within_hbm.1, bf16[512,512]{1,0:T(8,128)(2,1)} %across_hbm.1, ...), custom_call_target="tpu_custom_call" | custom-call | flops 8999999488 | bytes 12582912 | tf_op jit(solution)/shard_map/mixer/pallas_call | solution.py:291
  130.0 3.1 %copy.16 = bf16[16,128,512]{2,1,0:T(8,128)(2,1)} copy(bf16[16,128,512]{2,1,0:T(8,128)(2,1)} %mixer.1) | data formatting | bytes 4194304

commit v2 on v1

--- a/solution.py
+++ b/solution.py
@@ -30,40 +30,52 @@
     return h * cdf
 
 
+def div(n, d):
+    return n // d if isinstance(n, int) else lax.div(n, jnp.int32(d))
+
+
+def mod(n, d):
+    return n % d if isinstance(n, int) else lax.rem(n, jnp.int32(d))
+
+
 def place(x, z, y, core):
-    return x * 2 + z // 4, (z % 4) * 8 + y * 2 + core
+    return x * 2 + div(z, 4), mod(z, 4) * 8 + y * 2 + core
 
 
 def kernel(
     stream_hbm, wv_hbm, wg_hbm, wo_hbm, within_hbm, across_hbm, ws_hbm, as_hbm,
     mix_hbm, final_hbm, up_hbm, down_hbm,
-    out_hbm,
+    result,
     stream, wv, wg, wo, within, across, ws, ascale, mix_gain, final_gain, up, down,
     wvt, wgt, wst, normed, gates,
-    send1, recv1, send2, recv2, send3, recv3, flip1, flip2, result,
-    in_sem, out_sem, s1, r1, s2, r2, s3, r3,
+    send1, recv1, send2, recv2, send3, recv3, flip1, flip2,
+    in_sem, s1, r1, s2, r2, s3, r3,
 ):
     chan = lax.axis_index("chan")
     seq = lax.axis_index("seq")
-    x, z = chan // 2, (chan % 2) * 4 + seq // 8
-    y, core = (seq // 2) % 4, seq % 2
-    zl, yc = seq // 8, seq % 8
+    x, z = div(chan, 2), mod(chan, 2) * 4 + div(seq, 8)
+    y, core = mod(div(seq, 2), 4), mod(seq, 2)
+    zl, yc = div(seq, 8), mod(seq, 8)
     own = x * 8 + z
 
     def p_block(half, y_of, core_of):
-        return 2 * ((x + y_of + 2 * core_of + half) % NX) + core_of
+        return 2 * mod(x + y_of + 2 * core_of + half, NX) + core_of
 
     def load(number, source, target):
         return pltpu.make_async_copy(source, target, in_sem.at[number])
 
     loads = [
-        load(0, stream_hbm, stream), load(1, wv_hbm, wv), load(2, mix_hbm, mix_gain),
+        load(1, wv_hbm, wv), load(2, mix_hbm, mix_gain),
         load(3, wg_hbm, wg), load(4, within_hbm, within), load(5, ws_hbm, ws),
         load(6, across_hbm, across), load(7, as_hbm, ascale), load(8, wo_hbm, wo),
         load(9, final_hbm, final_gain), load(10, up_hbm, up), load(11, down_hbm, down),
     ]
-    for one in loads:
-        one.start()
+    loads = dict(zip(range(1, 12), loads))
+    for part in range(2):
+        rows = pl.ds(8 * part, 8)
+        loads[12 + part] = load(12 + part, stream_hbm.at[rows], stream.at[rows])
+    for number in (1, 12, 13, 2, 3, 4, 5, 6, 7, 8, 9, 10, 11):
+        loads[number].start()
 
     barrier = pltpu.get_barrier_semaphore()
 
@@ -74,57 +86,63 @@
 
     @pl.loop(1, NX * NZ)
     def _(i):
-        greet((x + i // NZ) % NX, (z + i % NZ) % NZ, y, core)
+        greet(mod(x + div(i, NZ), NX), mod(z + mod(i, NZ), NZ), y, core)
 
     @pl.loop(1, NY * NC)
     def _(i):
-        greet(x, z, (y + i // NC) % NY, (core + i % NC) % NC)
+        greet(x, z, mod(y + div(i, NC), NY), mod(core + mod(i, NC), NC))
 
     for half in range(2):
         @pl.loop(0, NX * NZ)
         def _(i):
-            x_of = i // NZ
-            core_of = chan % 2
-            greet(x_of, i % NZ, (x - x_of - 2 * core_of - half + 2 * NX) % NY, core_of)
+            x_of = div(i, NZ)
+            core_of = mod(chan, 2)
+            greet(x_of, mod(i, NZ), mod(x - x_of - 2 * core_of - half + 2 * NX, NY), core_of)
 
     for number in (1, 2):
         loads[number].wait()
     wvt[...] = wv[...].astype(F32).T.reshape(32, 2, 8, 512).swapaxes(0, 1).reshape(2, 256, 512).astype(BF16)
-    loads[0].wait()
-    gain = mix_gain[...].astype(F32)
+    gain = mix_gain[...].astype(F32).reshape(1, 512)
 
     def values(half, pair, tokens):
         found = dot(wvt[half], tokens, LAST)
         split = [found[:, :128].reshape(32, 8, 128), found[:, 128:].reshape(32, 8, 128)]
         send1[half, :, pair] = jnp.concatenate(split, axis=1).astype(BF16)
 
-    @pl.loop(0, 8)
-    def _(pair):
-        flat = stream[pl.ds(2 * pair, 2)].reshape(256, 512).astype(F32)
-        tokens = rms(flat, gain).astype(BF16)
-        normed[pair] = tokens
-        values(0, pair, tokens)
-
-    def send_values(half):
-        pltpu.make_async_copy(send1.at[half, own], recv1.at[half, chan, zl], r1.at[half]).start()
+    def send_values(half, first, count):
+        rows = pl.ds(first, count)
+        pltpu.make_async_copy(
+            send1.at[half, own, rows], recv1.at[half, chan, zl, rows], r1.at[half]
+        ).start()
 
         @pl.loop(1, NX * NZ)
         def _(i):
-            x_of, z_of = (x + i // NZ) % NX, (z + i % NZ) % NZ
+            x_of, z_of = mod(x + div(i, NZ), NX), mod(z + mod(i, NZ), NZ)
             pltpu.make_async_remote_copy(
-                send1.at[half, x_of * 8 + z_of], recv1.at[half, chan, zl],
+                send1.at[half, x_of * 8 + z_of, rows], recv1.at[half, chan, zl, rows],
                 s1.at[half], r1.at[half],
                 device_id=place(x_of, z_of, y, core), device_id_type=MESH,
             ).start()
 
-    pl.semaphore_wait(barrier, NX * NZ - 1 + NY * NC - 1 + 2 * NX * NZ)
-    send_values(0)
+    for part in range(2):
+        loads[12 + part].wait()
+
+        @pl.loop(4 * part, 4 * part + 4)
+        def _(pair):
+            flat = stream[pl.ds(2 * pair, 2)].reshape(256, 512).astype(F32)
+            tokens = rms(flat, gain).astype(BF16)
+            normed[pair] = tokens
+            values(0, pair, tokens)
+
+        if part == 0:
+            pl.semaphore_wait(barrier, NX * NZ - 1 + NY * NC - 1 + 2 * NX * NZ)
+        send_values(0, 4 * part, 4)
 
     @pl.loop(0, 8)
     def _(pair):
         values(1, pair, normed[pair])
 
-    send_values(1)
+    send_values(1, 0, 8)
 
     loads[3].wait()
     wgt[...] = wg[...].astype(F32).T.astype(BF16)
@@ -145,7 +163,7 @@
         edge = pl.ds(256 * n, 256)
         across[edge, edge] = jnp.where(lower, across[edge, edge].astype(F32), 0.0).astype(BF16)
     picked = lax.broadcasted_iota(jnp.int32, (16, 64), 1) == 16 * zl + lax.broadcasted_iota(jnp.int32, (16, 64), 0)
-    wst[...] = dot(picked.astype(F32).astype(BF16), ws[...], LAST)
+    wst[...] = dot(picked.astype(F32).astype(BF16), ws[...])
 
     def middle_of(half):
         pltpu.make_async_copy(recv1.at[half], recv1.at[half], r1.at[half]).wait()
@@ -163,14 +181,14 @@
                     column = flip1[side, pl.ds(c, 64, stride=8), :]
                     send2[half, 2 * n + side, c] = column.astype(BF16).reshape(4, 16, 128)
         pltpu.make_async_copy(
-            send2.at[half, p_block(half, y, core)], recv2.at[half, :, :, yc], r2.at[half]
+            send2.at[half, p_block(half, y, core)], recv2.at[half, yc], r2.at[half]
         ).start()
 
         @pl.loop(1, NY * NC)
         def _(i):
-            y_of, core_of = (y + i // NC) % NY, (core + i % NC) % NC
+            y_of, core_of = mod(y + div(i, NC), NY), mod(core + mod(i, NC), NC)
             pltpu.make_async_remote_copy(
-                send2.at[half, p_block(half, y_of, core_of)], recv2.at[half, :, :, yc],
+                send2.at[half, p_block(half, y_of, core_of)], recv2.at[half, yc],
                 s2.at[half], r2.at[half],
                 device_id=place(x, z, y_of, core_of), device_id_type=MESH,
             ).start()
@@ -179,7 +197,11 @@
         pltpu.make_async_copy(recv2.at[half], recv2.at[half], r2.at[half]).wait()
         for c in range(0, 8, 2):
             both = jnp.concatenate(
-                [recv2[half, c].reshape(512, 128), recv2[half, c + 1].reshape(512, 128)], axis=1
+                [
+                    jnp.concatenate([recv2[half, :, one, k].reshape(128, 128) for k in range(4)], axis=0)
+                    for one in (c, c + 1)
+                ],
+                axis=1,
             )
             row = lax.broadcasted_iota(jnp.int32, (64, 256), 0)
             wanted = 16 * zl + 8 * half + c + lax.broadcasted_iota(jnp.int32, (64, 256), 1) // 128
@@ -187,7 +209,7 @@
             for n in range(2):
                 rows = pl.ds(256 * n, 256)
                 found = dot(across[rows, pl.ds(0, 256 * (n + 1))], both[: 256 * (n + 1)])
-                found = found * dot(ascale[rows, :], spread)
+                found = found * dot(ascale[:, rows], spread, FIRST)
                 for side in range(2):
                     flip2[pl.ds(2048 * n + c + side, 256, stride=8), :] = found[:, 128 * side : 128 * side + 128]
 
@@ -201,17 +223,17 @@
         rows = pl.ds(first, count)
 
         def remote(i):
-            zl_of, yc_of = (zl + i % 4) % 4, (yc + i // 4) % 8
+            zl_of, yc_of = mod(zl + mod(i, 4), 4), mod(yc + div(i, 4), 8)
             seq_of = zl_of * 8 + yc_of
             pltpu.make_async_remote_copy(
-                send3.at[half, seq_of, rows], recv3.at[half, rows, own],
+                send3.at[half, seq_of, rows], recv3.at[half, own, rows],
                 s3.at[sem], r3.at[sem], device_id=(block, seq_of), device_id_type=MESH,
             ).start()
 
         @pl.when(block == chan)
         def _():
             pltpu.make_async_copy(
-                send3.at[half, seq, rows], recv3.at[half, rows, own], r3.at[sem]
+                send3.at[half, seq, rows], recv3.at[half, own, rows], r3.at[sem]
             ).start()
 
         @pl.when(block != chan)
@@ -231,14 +253,14 @@
         send_mixed(1, 2 * part, 2, part)
 
     pltpu.make_async_copy(recv3.at[0], recv3.at[0], r3.at[4]).wait()
-    gain2 = final_gain[...].astype(F32)
+    gain2 = final_gain[...].astype(F32).reshape(1, 512)
     for part in range(4):
-        arrived = recv3.at[1, pl.ds(2 * part, 2)]
+        arrived = recv3.at[1, :, pl.ds(2 * part, 2)]
         pltpu.make_async_copy(arrived, arrived, r3.at[part]).wait()
 
         @pl.loop(2 * part, 2 * part + 2)
         def _(pair):
-            halves = [recv3[half, pair].astype(F32) for half in range(2)]
+            halves = [recv3[half, :, pair].astype(F32) for half in range(2)]
             projected = []
             for one in range(2):
                 mixed = jnp.concatenate([h[:, 8 * one : 8 * one + 8] for h in halves], axis=1)
@@ -254,9 +276,6 @@
             total = (middle + jnp.concatenate(outer, axis=1)).astype(BF16)
             result[pl.ds(2 * pair, 2)] = total.reshape(2, 128, 512)
 
-        rows = pl.ds(4 * part, 4)
-        pltpu.make_async_copy(result.at[rows], out_hbm.at[rows], out_sem.at[part]).start()
-
     for half in range(2):
         sent = send1.at[half, pl.ds(0, 31)]
         pltpu.make_async_copy(sent, sent, s1.at[half]).wait()
@@ -273,10 +292,6 @@
             one = send3.at[half, 0, rows]
             pltpu.make_async_copy(one, one, s3.at[sem]).wait()
 
-    for part in range(4):
-        rows = pl.ds(4 * part, 4)
-        pltpu.make_async_copy(result.at[rows], out_hbm.at[rows], out_sem.at[part]).wait()
-
 
 def body(
     stream, weight_value, weight_gate, weight_out, within_factor, across_factor,
@@ -284,15 +299,15 @@
 ):
     args = (
         stream, weight_value, weight_gate, weight_out, within_factor, across_factor,
-        within_scale, across_scale, mix_gain.reshape(1, -1), final_gain.reshape(1, -1),
+        within_scale.T, across_scale.T, mix_gain, final_gain,
         block_up, block_down,
     )
     anywhere = pl.BlockSpec(memory_space=pl.ANY)
     return pl.pallas_call(
         kernel,
-        out_shape=jax.ShapeDtypeStruct(stream.shape, BF16),
+        out_shape=pltpu.VMEM(stream.shape, BF16),
         in_specs=[anywhere] * len(args),
-        out_specs=anywhere,
+        out_specs=pl.BlockSpec(memory_space=pltpu.VMEM),
         scratch_shapes=[pltpu.VMEM(a.shape, BF16) for a in args] + [
             pltpu.VMEM((2, 256, 512), BF16),
             pltpu.VMEM((512, 512), BF16),
@@ -302,14 +317,12 @@
             pltpu.VMEM((2, 32, 8, 16, 128), BF16),
             pltpu.VMEM((2, 8, 4, 8, 16, 128), BF16),
             pltpu.VMEM((2, 8, 8, 4, 16, 128), BF16),
-            pltpu.VMEM((2, 8, 4, 8, 16, 128), BF16),
+            pltpu.VMEM((2, 8, 8, 4, 16, 128), BF16),
             pltpu.VMEM((2, 32, 8, 16, 128), BF16),
-            pltpu.VMEM((2, 8, 32, 16, 128), BF16),
+            pltpu.VMEM((2, 32, 8, 16, 128), BF16),
             pltpu.VMEM((2, 512, 128), F32),
             pltpu.VMEM((4096, 128), F32),
-            pltpu.VMEM((16, 128, 512), BF16),
-            pltpu.SemaphoreType.DMA((12,)),
-            pltpu.SemaphoreType.DMA((4,)),
+            pltpu.SemaphoreType.DMA((14,)),
             pltpu.SemaphoreType.DMA((2,)),
             pltpu.SemaphoreType.DMA((2,)),
             pltpu.SemaphoreType.DMA((2,)),

time: 133 us -> 125 us (0.940)
  local copies, waits for them, and re-layouts: 8.96 us -> 1.32 us
    unnamed x3 -> x1, local copies, waits for them, and re-layouts: 6.43 us -> 1.32 us
    reshape x2 -> x0, local copies, waits for them, and re-layouts: 2.53 us -> none  [the longest x1 1.27 us: body(): mix_gain.reshape(1, -1)]
where the time goes in v2:
time: 125 us
  Pallas kernels  124 us (99%)
  local copies, waits for them, and re-layouts  1.32 us (1%)
    pallas_call x1, Pallas kernels, body(): pl.pallas_call(kernel, out_shape=pltpu.VMEM(stream.shape, BF16), in_specs...  124 us

profile of v2, /device:TPU:1, one launch (start us, length us, event | category | flops | bytes accessed | tf_op | source)
XLA Modules:
  0.0 125.1 jit_solution(4906241532121267947)
XLA Ops:
  0.0 123.8 %mixer.1 = bf16[16,128,512]{2,1,0:T(8,128)(2,1)S(1)} custom-call(bf16[16,128,512]{2,1,0:T(8,128)(2,1)} %stream_hbm.1, bf16[512,512]{1,0:T(8,128)(2,1)} %wv_hbm.1, bf16[512,512]{1,0:T(8,128)(2,1)} %wg_hbm.1, bf16[512,512]{1,0:T(8,128)(2,1)} %wo_hbm.1, bf16[1024,1024]{1,0:T(8,128)(2,1)} %within_hbm.1, bf16[512,512]{1,0:T(8,128)(2,1)} %across_hbm.1, ...), custom_call_target="tpu_custom_call" | custom-call | flops 8999999488 | bytes 12582912 | tf_op jit(solution)/shard_map/mixer/pallas_call | solution.py:306
  123.8 1.3 %copy.14 = bf16[16,128,512]{2,1,0:T(8,128)(2,1)} copy(bf16[16,128,512]{2,1,0:T(8,128)(2,1)S(1)} %mixer.1) | data formatting | bytes 4194304

commit v3 on v2

--- a/solution.py
+++ b/solution.py
@@ -9,6 +9,9 @@
 MESH = pl.DeviceIdType.MESH
 F32 = jnp.float32
 BF16 = jnp.bfloat16
+GT = jnp.bfloat16
+PARTS = 4
+PP = 8 // PARTS
 NX, NZ, NY, NC = 4, 8, 4, 2
 LAST = (((1,), (1,)), ((), ()))
 FIRST = (((0,), (0,)), ((), ()))
@@ -26,8 +29,14 @@
 
 
 def gelu(h):
-    cdf = 0.5 * (1.0 + jnp.tanh(0.7978845608028654 * (h + 0.044715 * (h * h * h))))
-    return h * cdf
+    bent = jnp.tanh(h * (0.7978845608028654 + 0.035677408136300125 * (h * h)))
+    half = 0.5 * h
+    return half + half * bent
+
+
+def halves_first(weight, axis_rows):
+    grouped = weight.reshape(32, 2, 8, axis_rows).swapaxes(0, 1)
+    return grouped.reshape(2, 256, axis_rows).astype(BF16)
 
 
 def div(n, d):
@@ -47,7 +56,7 @@
     mix_hbm, final_hbm, up_hbm, down_hbm,
     result,
     stream, wv, wg, wo, within, across, ws, ascale, mix_gain, final_gain, up, down,
-    wvt, wgt, wst, normed, gates,
+    wvt, wgt, wot, partial, wst, normed, gates,
     send1, recv1, send2, recv2, send3, recv3, flip1, flip2,
     in_sem, s1, r1, s2, r2, s3, r3,
 ):
@@ -101,7 +110,7 @@
 
     for number in (1, 2):
         loads[number].wait()
-    wvt[...] = wv[...].astype(F32).T.reshape(32, 2, 8, 512).swapaxes(0, 1).reshape(2, 256, 512).astype(BF16)
+    wvt[...] = halves_first(wv[...].astype(F32).T, 512)
     gain = mix_gain[...].astype(F32).reshape(1, 512)
 
     def values(half, pair, tokens):
@@ -145,15 +154,19 @@
     send_values(1, 0, 8)
 
     loads[3].wait()
-    wgt[...] = wg[...].astype(F32).T.astype(BF16)
+    wgt[...] = halves_first(wg[...].astype(F32).T, 512)
 
     @pl.loop(0, 8)
     def _(pair):
-        found = dot(wgt[...], normed[pair], LAST).astype(BF16)
-        gates[2 * pair] = found[:, :128]
-        gates[2 * pair + 1] = found[:, 128:]
-
-    for number in range(4, 12):
+        for half in range(2):
+            found = dot(wgt[half], normed[pair], LAST).astype(BF16)
+            gates[half, 2 * pair] = found[:, :128]
+            gates[half, 2 * pair + 1] = found[:, 128:]
+
+    loads[8].wait()
+    wot[...] = halves_first(wo[...].astype(F32), 512)
+
+    for number in (4, 5, 6, 7, 9, 10, 11):
         loads[number].wait()
     lower = lax.broadcasted_iota(jnp.int32, (256, 256), 0) >= lax.broadcasted_iota(jnp.int32, (256, 256), 1)
     for n in range(4):
@@ -246,44 +259,50 @@
 
     middle_of(0)
     across_of(0)
-    send_mixed(0, 0, 8, 4)
+    send_mixed(0, 0, 8, PARTS)
     middle_of(1)
     across_of(1)
-    for part in range(4):
-        send_mixed(1, 2 * part, 2, part)
-
-    pltpu.make_async_copy(recv3.at[0], recv3.at[0], r3.at[4]).wait()
+    for part in range(PARTS):
+        send_mixed(1, PP * part, PP, part)
+
+    pltpu.make_async_copy(recv3.at[0], recv3.at[0], r3.at[PARTS]).wait()
+
+    def projected(half, pair):
+        mixed = recv3[half, :, pair].astype(F32)
+        gated = [
+            (mixed[:, 8 * one : 8 * one + 8].reshape(256, 128) * gates[half, 2 * pair + one].astype(F32)).astype(BF16)
+            for one in range(2)
+        ]
+        return dot(jnp.concatenate(gated, axis=1), wot[half], FIRST)
+
+    @pl.loop(0, 8)
+    def _(pair):
+        flat = stream[pl.ds(2 * pair, 2)].reshape(256, 512).astype(F32)
+        partial[pair] = flat + projected(0, pair)
+
     gain2 = final_gain[...].astype(F32).reshape(1, 512)
-    for part in range(4):
-        arrived = recv3.at[1, :, pl.ds(2 * part, 2)]
+    for part in range(PARTS):
+        arrived = recv3.at[1, :, pl.ds(PP * part, PP)]
         pltpu.make_async_copy(arrived, arrived, r3.at[part]).wait()
-
-        @pl.loop(2 * part, 2 * part + 2)
-        def _(pair):
-            halves = [recv3[half, :, pair].astype(F32) for half in range(2)]
-            projected = []
-            for one in range(2):
-                mixed = jnp.concatenate([h[:, 8 * one : 8 * one + 8] for h in halves], axis=1)
-                gated = mixed.reshape(512, 128) * gates[2 * pair + one].astype(F32)
-                projected.append(dot(gated.astype(BF16), wo[...], FIRST))
-            flat = stream[pl.ds(2 * pair, 2)].reshape(256, 512).astype(F32)
-            middle = (flat + jnp.concatenate(projected, axis=0)).astype(BF16).astype(F32)
-            renormed = rms(middle, gain2).astype(BF16)
-            outer = []
-            for k in range(4):
-                inner = gelu(dot(renormed[:, 128 * k : 128 * k + 128], up[k])).astype(BF16)
-                outer.append(dot(inner, down[k]))
-            total = (middle + jnp.concatenate(outer, axis=1)).astype(BF16)
-            result[pl.ds(2 * pair, 2)] = total.reshape(2, 128, 512)
+        pairs = range(PP * part, PP * part + PP)
+        middle = jnp.concatenate([partial[pair] + projected(1, pair) for pair in pairs], axis=0)
+        middle = middle.astype(BF16).astype(F32)
+        renormed = rms(middle, gain2).astype(BF16)
+        outer = []
+        for k in range(4):
+            inner = gelu(dot(renormed[:, 128 * k : 128 * k + 128], up[k]).astype(GT)).astype(BF16)
+            outer.append(dot(inner, down[k]))
+        total = (middle + jnp.concatenate(outer, axis=1)).astype(BF16)
+        result[pl.ds(2 * PP * part, 2 * PP)] = total.reshape(2 * PP, 128, 512)
 
     for half in range(2):
         sent = send1.at[half, pl.ds(0, 31)]
         pltpu.make_async_copy(sent, sent, s1.at[half]).wait()
         sent = send2.at[half, pl.ds(0, 7)]
         pltpu.make_async_copy(sent, sent, s2.at[half]).wait()
-    for sem in range(5):
-        rows = pl.ds(0, 8) if sem == 4 else pl.ds(2 * sem, 2)
-        half = 0 if sem == 4 else 1
+    for sem in range(PARTS + 1):
+        rows = pl.ds(0, 8) if sem == PARTS else pl.ds(PP * sem, PP)
+        half = 0 if sem == PARTS else 1
         rest = send3.at[half, pl.ds(1, 31), rows]
         pltpu.make_async_copy(rest, rest, s3.at[sem]).wait()
 
@@ -310,10 +329,12 @@
         out_specs=pl.BlockSpec(memory_space=pltpu.VMEM),
         scratch_shapes=[pltpu.VMEM(a.shape, BF16) for a in args] + [
             pltpu.VMEM((2, 256, 512), BF16),
-            pltpu.VMEM((512, 512), BF16),
+            pltpu.VMEM((2, 256, 512), BF16),
+            pltpu.VMEM((2, 256, 512), BF16),
+            pltpu.VMEM((8, 256, 512), F32),
             pltpu.VMEM((16, 1024), F32),
             pltpu.VMEM((8, 256, 512), BF16),
-            pltpu.VMEM((16, 512, 128), BF16),
+            pltpu.VMEM((2, 16, 256, 128), BF16),
             pltpu.VMEM((2, 32, 8, 16, 128), BF16),
             pltpu.VMEM((2, 8, 4, 8, 16, 128), BF16),
             pltpu.VMEM((2, 8, 8, 4, 16, 128), BF16),
@@ -327,8 +348,8 @@
             pltpu.SemaphoreType.DMA((2,)),
             pltpu.SemaphoreType.DMA((2,)),
             pltpu.SemaphoreType.DMA((2,)),
-            pltpu.SemaphoreType.DMA((5,)),
-            pltpu.SemaphoreType.DMA((5,)),
+            pltpu.SemaphoreType.DMA((PARTS + 1,)),
+            pltpu.SemaphoreType.DMA((PARTS + 1,)),
         ],
         compiler_params=pltpu.CompilerParams(
             collective_id=0, has_side_effects=True, vmem_limit_bytes=56 * 2**20

time: 125 us -> 119 us (0.952)
  Pallas kernels: 124 us -> 117 us
    pallas_call x1, Pallas kernels: 124 us -> 117 us  [body(): pl.pallas_call(kernel, out_shape=pltpu.VMEM(stream.shape, BF16), in_specs...]
where the time goes in v3:
time: 119 us
  Pallas kernels  117 us (98%)
  local copies, waits for them, and re-layouts  1.32 us (1%)
    pallas_call x1, Pallas kernels, body(): pl.pallas_call(kernel, out_shape=pltpu.VMEM(stream.shape, BF16), in_specs...  117 us

profile of v3, /device:TPU:1, one launch (start us, length us, event | category | flops | bytes accessed | tf_op | source)
XLA Modules:
  0.0 118.6 jit_solution(14623499933274346317)
XLA Ops:
  0.0 117.2 %mixer.1 = bf16[16,128,512]{2,1,0:T(8,128)(2,1)S(1)} custom-call(bf16[16,128,512]{2,1,0:T(8,128)(2,1)} %stream_hbm.1, bf16[512,512]{1,0:T(8,128)(2,1)} %wv_hbm.1, bf16[512,512]{1,0:T(8,128)(2,1)} %wg_hbm.1, bf16[512,512]{1,0:T(8,128)(2,1)} %wo_hbm.1, bf16[1024,1024]{1,0:T(8,128)(2,1)} %within_hbm.1, bf16[512,512]{1,0:T(8,128)(2,1)} %across_hbm.1, ...), custom_call_target="tpu_custom_call" | custom-call | flops 8999999488 | bytes 12582912 | tf_op jit(solution)/shard_map/mixer/pallas_call | solution.py:325
  117.2 1.3 %copy.14 = bf16[16,128,512]{2,1,0:T(8,128)(2,1)} copy(bf16[16,128,512]{2,1,0:T(8,128)(2,1)S(1)} %mixer.1) | data formatting | bytes 4194304

commit v4 on v3

--- a/solution.py
+++ b/solution.py
@@ -10,6 +10,7 @@
 F32 = jnp.float32
 BF16 = jnp.bfloat16
 GT = jnp.bfloat16
+MAPH = 0
 PARTS = 4
 PP = 8 // PARTS
 NX, NZ, NY, NC = 4, 8, 4, 2
@@ -68,7 +69,7 @@
     own = x * 8 + z
 
     def p_block(half, y_of, core_of):
-        return 2 * mod(x + y_of + 2 * core_of + half, NX) + core_of
+        return 2 * mod(x + y_of + 2 * core_of + half, NX) + mod(core_of + MAPH * half, NC)
 
     def load(number, source, target):
         return pltpu.make_async_copy(source, target, in_sem.at[number])
@@ -105,7 +106,7 @@
         @pl.loop(0, NX * NZ)
         def _(i):
             x_of = div(i, NZ)
-            core_of = mod(chan, 2)
+            core_of = mod(chan + MAPH * half, NC)
             greet(x_of, mod(i, NZ), mod(x - x_of - 2 * core_of - half + 2 * NX, NY), core_of)
 
     for number in (1, 2):
@@ -118,40 +119,41 @@
         split = [found[:, :128].reshape(32, 8, 128), found[:, 128:].reshape(32, 8, 128)]
         send1[half, :, pair] = jnp.concatenate(split, axis=1).astype(BF16)
 
-    def send_values(half, first, count):
-        rows = pl.ds(first, count)
+    def send_values(half, block):
+        rows = pl.ds(4 * block, 4)
         pltpu.make_async_copy(
-            send1.at[half, own, rows], recv1.at[half, chan, zl, rows], r1.at[half]
+            send1.at[half, own, rows], recv1.at[half, block, chan, zl], r1.at[half, block]
         ).start()
 
         @pl.loop(1, NX * NZ)
         def _(i):
             x_of, z_of = mod(x + div(i, NZ), NX), mod(z + mod(i, NZ), NZ)
             pltpu.make_async_remote_copy(
-                send1.at[half, x_of * 8 + z_of, rows], recv1.at[half, chan, zl, rows],
-                s1.at[half], r1.at[half],
+                send1.at[half, x_of * 8 + z_of, rows], recv1.at[half, block, chan, zl],
+                s1.at[half], r1.at[half, block],
                 device_id=place(x_of, z_of, y, core), device_id_type=MESH,
             ).start()
 
-    for part in range(2):
-        loads[12 + part].wait()
-
-        @pl.loop(4 * part, 4 * part + 4)
+    for block in range(2):
+        loads[12 + block].wait()
+
+        @pl.loop(4 * block, 4 * block + 4)
         def _(pair):
             flat = stream[pl.ds(2 * pair, 2)].reshape(256, 512).astype(F32)
             tokens = rms(flat, gain).astype(BF16)
             normed[pair] = tokens
             values(0, pair, tokens)
 
-        if part == 0:
+        if block == 0:
             pl.semaphore_wait(barrier, NX * NZ - 1 + NY * NC - 1 + 2 * NX * NZ)
-        send_values(0, 4 * part, 4)
-
-    @pl.loop(0, 8)
-    def _(pair):
-        values(1, pair, normed[pair])
-
-    send_values(1, 0, 8)
+        send_values(0, block)
+
+    for block in range(2):
+        @pl.loop(4 * block, 4 * block + 4)
+        def _(pair):
+            values(1, pair, normed[pair])
+
+        send_values(1, block)
 
     loads[3].wait()
     wgt[...] = halves_first(wg[...].astype(F32).T, 512)
@@ -175,33 +177,41 @@
     for n in range(2):
         edge = pl.ds(256 * n, 256)
         across[edge, edge] = jnp.where(lower, across[edge, edge].astype(F32), 0.0).astype(BF16)
+    old = lax.broadcasted_iota(jnp.int32, (256, 256), 0)
+    new = lax.broadcasted_iota(jnp.int32, (256, 256), 1)
+    moved = (old & 119) + ((old >> 3) & 1) * 128 + (old >> 7) * 8
+    swap = (moved == new).astype(F32).astype(BF16)
+    for n in range(2):
+        edge = pl.ds(256 * n, 256)
+        across[:, edge] = dot(across[:, edge], swap).astype(BF16)
     picked = lax.broadcasted_iota(jnp.int32, (16, 64), 1) == 16 * zl + lax.broadcasted_iota(jnp.int32, (16, 64), 0)
     wst[...] = dot(picked.astype(F32).astype(BF16), ws[...])
 
-    def middle_of(half):
-        pltpu.make_async_copy(recv1.at[half], recv1.at[half], r1.at[half]).wait()
+    def middle_of(half, block):
+        arrived = recv1.at[half, block]
+        pltpu.make_async_copy(arrived, arrived, r1.at[half, block]).wait()
         for n in range(4):
-            blocks = [recv1[half, k].reshape(512, 128) for k in range(2 * n + 2)]
+            blocks = [recv1[half, block, k].reshape(256, 128) for k in range(2 * n + 2)]
             found = dot(
                 jnp.concatenate(blocks, axis=1), within[pl.ds(256 * n, 256), pl.ds(0, 256 * (n + 1))], LAST
             )
             scale = wst[pl.ds(8 * half, 8), pl.ds(256 * n, 256)]
-            scaled = (found.reshape(64, 8, 256) * scale[None]).reshape(512, 256)
+            scaled = (found.reshape(32, 8, 256) * scale[None]).reshape(256, 256)
             for side in range(2):
-                flip1[side] = scaled[:, 128 * side : 128 * side + 128]
+                flip1[n, side] = scaled[:, 128 * side : 128 * side + 128]
             for side in range(2):
                 for c in range(8):
-                    column = flip1[side, pl.ds(c, 64, stride=8), :]
-                    send2[half, 2 * n + side, c] = column.astype(BF16).reshape(4, 16, 128)
+                    column = flip1[n, side, pl.ds(c, 32, stride=8), :]
+                    send2[half, block, 2 * n + side, c] = column.astype(BF16).reshape(2, 16, 128)
         pltpu.make_async_copy(
-            send2.at[half, p_block(half, y, core)], recv2.at[half, yc], r2.at[half]
+            send2.at[half, block, p_block(half, y, core)], recv2.at[half, block, yc], r2.at[half]
         ).start()
 
         @pl.loop(1, NY * NC)
         def _(i):
             y_of, core_of = mod(y + div(i, NC), NY), mod(core + mod(i, NC), NC)
             pltpu.make_async_remote_copy(
-                send2.at[half, p_block(half, y_of, core_of)], recv2.at[half, yc],
+                send2.at[half, block, p_block(half, y_of, core_of)], recv2.at[half, block, yc],
                 s2.at[half], r2.at[half],
                 device_id=place(x, z, y_of, core_of), device_id_type=MESH,
             ).start()
@@ -211,7 +221,11 @@
         for c in range(0, 8, 2):
             both = jnp.concatenate(
                 [
-                    jnp.concatenate([recv2[half, :, one, k].reshape(128, 128) for k in range(4)], axis=0)
+                    jnp.concatenate([
+                            recv2[half, block, :, one, k].reshape(128, 128)
+                            for k in range(2)
+                            for block in range(2)
+                        ], axis=0)
                     for one in (c, c + 1)
                 ],
                 axis=1,
@@ -257,10 +271,12 @@
         def _(i):
             remote(i)
 
-    middle_of(0)
+    middle_of(0, 0)
+    middle_of(0, 1)
     across_of(0)
     send_mixed(0, 0, 8, PARTS)
-    middle_of(1)
+    middle_of(1, 0)
+    middle_of(1, 1)
     across_of(1)
     for part in range(PARTS):
         send_mixed(1, PP * part, PP, part)
@@ -298,7 +314,7 @@
     for half in range(2):
         sent = send1.at[half, pl.ds(0, 31)]
         pltpu.make_async_copy(sent, sent, s1.at[half]).wait()
-        sent = send2.at[half, pl.ds(0, 7)]
+        sent = send2.at[half, :, pl.ds(0, 7)]
         pltpu.make_async_copy(sent, sent, s2.at[half]).wait()
     for sem in range(PARTS + 1):
         rows = pl.ds(0, 8) if sem == PARTS else pl.ds(PP * sem, PP)
@@ -336,16 +352,16 @@
             pltpu.VMEM((8, 256, 512), BF16),
             pltpu.VMEM((2, 16, 256, 128), BF16),
             pltpu.VMEM((2, 32, 8, 16, 128), BF16),
-            pltpu.VMEM((2, 8, 4, 8, 16, 128), BF16),
-            pltpu.VMEM((2, 8, 8, 4, 16, 128), BF16),
-            pltpu.VMEM((2, 8, 8, 4, 16, 128), BF16),
+            pltpu.VMEM((2, 2, 8, 4, 4, 16, 128), BF16),
+            pltpu.VMEM((2, 2, 8, 8, 2, 16, 128), BF16),
+            pltpu.VMEM((2, 2, 8, 8, 2, 16, 128), BF16),
             pltpu.VMEM((2, 32, 8, 16, 128), BF16),
             pltpu.VMEM((2, 32, 8, 16, 128), BF16),
-            pltpu.VMEM((2, 512, 128), F32),
+            pltpu.VMEM((4, 2, 256, 128), F32),
             pltpu.VMEM((4096, 128), F32),
             pltpu.SemaphoreType.DMA((14,)),
             pltpu.SemaphoreType.DMA((2,)),
-            pltpu.SemaphoreType.DMA((2,)),
+            pltpu.SemaphoreType.DMA((2, 2)),
             pltpu.SemaphoreType.DMA((2,)),
             pltpu.SemaphoreType.DMA((2,)),
             pltpu.SemaphoreType.DMA((PARTS + 1,)),

time: 119 us -> 111 us (0.933)
  Pallas kernels: 117 us -> 110 us
    pallas_call x1, Pallas kernels: 117 us -> 110 us  [body(): pl.pallas_call(kernel, out_shape=pltpu.VMEM(stream.shape, BF16), in_specs...]
where the time goes in v4:
time: 111 us
  Pallas kernels  110 us (99%)
  local copies, waits for them, and re-layouts  1.32 us (1%)
    pallas_call x1, Pallas kernels, body(): pl.pallas_call(kernel, out_shape=pltpu.VMEM(stream.shape, BF16), in_specs...  110 us

profile of v4, /device:TPU:1, one launch (start us, length us, event | category | flops | bytes accessed | tf_op | source)
XLA Modules:
  0.0 111.3 jit_solution(13624255849262006270)
XLA Ops:
  0.0 110.0 %mixer.1 = bf16[16,128,512]{2,1,0:T(8,128)(2,1)S(1)} custom-call(bf16[16,128,512]{2,1,0:T(8,128)(2,1)} %stream_hbm.1, bf16[512,512]{1,0:T(8,128)(2,1)} %wv_hbm.1, bf16[512,512]{1,0:T(8,128)(2,1)} %wg_hbm.1, bf16[512,512]{1,0:T(8,128)(2,1)} %wo_hbm.1, bf16[1024,1024]{1,0:T(8,128)(2,1)} %within_hbm.1, bf16[512,512]{1,0:T(8,128)(2,1)} %across_hbm.1, ...), custom_call_target="tpu_custom_call" | custom-call | flops 8999999488 | bytes 12582912 | tf_op jit(solution)/shard_map/mixer/pallas_call | solution.py:341
  110.0 1.3 %copy.14 = bf16[16,128,512]{2,1,0:T(8,128)(2,1)} copy(bf16[16,128,512]{2,1,0:T(8,128)(2,1)S(1)} %mixer.1) | data formatting | bytes 4194304

commit v5 on v4

--- a/solution.py
+++ b/solution.py
@@ -10,7 +10,6 @@
 F32 = jnp.float32
 BF16 = jnp.bfloat16
 GT = jnp.bfloat16
-MAPH = 0
 PARTS = 4
 PP = 8 // PARTS
 NX, NZ, NY, NC = 4, 8, 4, 2
@@ -69,7 +68,7 @@
     own = x * 8 + z
 
     def p_block(half, y_of, core_of):
-        return 2 * mod(x + y_of + 2 * core_of + half, NX) + mod(core_of + MAPH * half, NC)
+        return 2 * mod(x + y_of + 2 * core_of + half, NX) + core_of
 
     def load(number, source, target):
         return pltpu.make_async_copy(source, target, in_sem.at[number])
@@ -102,12 +101,6 @@
     def _(i):
         greet(x, z, mod(y + div(i, NC), NY), mod(core + mod(i, NC), NC))
 
-    for half in range(2):
-        @pl.loop(0, NX * NZ)
-        def _(i):
-            x_of = div(i, NZ)
-            core_of = mod(chan + MAPH * half, NC)
-            greet(x_of, mod(i, NZ), mod(x - x_of - 2 * core_of - half + 2 * NX, NY), core_of)
 
     for number in (1, 2):
         loads[number].wait()
@@ -145,7 +138,7 @@
             values(0, pair, tokens)
 
         if block == 0:
-            pl.semaphore_wait(barrier, NX * NZ - 1 + NY * NC - 1 + 2 * NX * NZ)
+            pl.semaphore_wait(barrier, NX * NZ - 1 + NY * NC - 1)
         send_values(0, block)
 
     for block in range(2):

time: 111 us -> 108 us (0.973)
  Pallas kernels: 110 us -> 107 us
    pallas_call x1, Pallas kernels: 110 us -> 107 us  [body(): pl.pallas_call(kernel, out_shape=pltpu.VMEM(stream.shape, BF16), in_specs...]
where the time goes in v5:
time: 108 us
  Pallas kernels  107 us (99%)
  local copies, waits for them, and re-layouts  1.32 us (1%)
    pallas_call x1, Pallas kernels, body(): pl.pallas_call(kernel, out_shape=pltpu.VMEM(stream.shape, BF16), in_specs...  107 us

profile of v5, /device:TPU:1, one launch (start us, length us, event | category | flops | bytes accessed | tf_op | source)
XLA Modules:
  0.0 108.0 jit_solution(8669486420920382241)
XLA Ops:
  0.0 106.6 %mixer.1 = bf16[16,128,512]{2,1,0:T(8,128)(2,1)S(1)} custom-call(bf16[16,128,512]{2,1,0:T(8,128)(2,1)} %stream_hbm.1, bf16[512,512]{1,0:T(8,128)(2,1)} %wv_hbm.1, bf16[512,512]{1,0:T(8,128)(2,1)} %wg_hbm.1, bf16[512,512]{1,0:T(8,128)(2,1)} %wo_hbm.1, bf16[1024,1024]{1,0:T(8,128)(2,1)} %within_hbm.1, bf16[512,512]{1,0:T(8,128)(2,1)} %across_hbm.1, ...), custom_call_target="tpu_custom_call" | custom-call | flops 8999999488 | bytes 12582912 | tf_op jit(solution)/shard_map/mixer/pallas_call | solution.py:334
  106.6 1.3 %copy.14 = bf16[16,128,512]{2,1,0:T(8,128)(2,1)} copy(bf16[16,128,512]{2,1,0:T(8,128)(2,1)S(1)} %mixer.1) | data formatting | bytes 4194304
